TPU v7x, 32 devices: a whole 2x2x4 slice. The times are simulated.
32 devices in a mesh: group: 2 (over y), seq: 16 (over z, x, core).
Axes of the slice: x: 2, y: 2, z: 4, core: 2. Of those that a mesh axis runs over, the one named last changes fastest.
Arguments:
- prompt_queries: bfloat16 [2048, 4096], P(('group', 'seq')), parts along dimension 0, may hold values from -80 to 80
- prompt_keys: bfloat16 [2048, 512], P(('group', 'seq')), parts along dimension 0, may hold values from -4 to 4
- prompt_values: bfloat16 [2048, 512], P(('group', 'seq')), parts along dimension 0, may hold values from -5 to 5
- prompt_positions: int32 [2048], P(('group', 'seq')), parts along dimension 0, may hold values from 0 to 1023, as said below
- step_queries: bfloat16 [32, 2, 4096], P(('group', 'seq')), parts along dimension 0, may hold values from -80 to 80
- step_keys: bfloat16 [32, 2, 512], P(('group', 'seq')), parts along dimension 0, may hold values from -5 to 5
- step_values: bfloat16 [32, 2, 512], P(('group', 'seq')), parts along dimension 0, may hold values from -5 to 5
- pool_keys: bfloat16 [1024, 128, 512], P(('group', 'seq')), parts along dimension 0, may hold values from -4 to 4
- pool_values: bfloat16 [1024, 128, 512], P(('group', 'seq')), parts along dimension 0, may hold values from -5 to 5
- page_owner: int32 [1024, 1], P(('group', 'seq')), parts along dimension 0, may hold values from 0 to 15
- page_fill: int32 [1024], P(('group', 'seq')), parts along dimension 0, may hold values from 1 to 128
Outputs:
- prefill_out: bfloat16 [2048, 4096], P(('group', 'seq')), parts along dimension 0
- decode_out: bfloat16 [32, 2, 4096], P(('group', 'seq')), parts along dimension 0
There are 2 independent parts, one for each index of `group`. A program takes and returns all parts, laid end to end along the dimension named above; each array names one. Nothing has to cross between parts.
Inputs may be any that keep to these rules, and one draw needn't show every extreme that they name: `prompt_positions`: each device's 64 rows are two runs of consecutive positions, each of half of 64 rows and starting at a multiple of that half; every position of 0 to 1023 appears once. `page_owner`: every decode sequence owns at least one page.
All inputs are finite; a program needn't handle non-finite values.
Results may differ from a plain program's by a relative error of at most 0.009.
Values may be sent and summed in bfloat16 or wider, within the bound.
A program may use at most 192 MiB of HBM per device.

v0:
```python
import jax
import jax.numpy as jnp
from jax import lax
from jax.sharding import PartitionSpec as P

QH = 32
KVH = 4
HD = 128
PAGE = 128
STEPS = 2


NEG_FILL = -1e30


def finish_steps(own_queries, own_keys, own_values, own_max, own_sum, own_total):
    seq_count = own_queries.shape[0]
    group_size = QH // KVH
    query_heads = own_queries.reshape(seq_count, STEPS, KVH, group_size, HD)
    key_heads = own_keys.reshape(seq_count, STEPS, KVH, HD)
    value_heads = own_values.astype(jnp.float32).reshape(seq_count, STEPS, KVH, HD)
    step_scores = jnp.einsum(
        "bskgd,bjkd->bskgj", query_heads, key_heads, preferred_element_type=jnp.float32
    ) * HD ** (-0.5)
    step_mask = jnp.arange(STEPS)[None, :] <= jnp.arange(STEPS)[:, None]
    mask_full = step_mask[None, :, None, None, :]
    step_scores = jnp.where(mask_full, step_scores, NEG_FILL)
    overall = jnp.maximum(own_max, jnp.max(step_scores, axis=-1))
    pool_scale = jnp.exp(own_max - overall)
    step_weights = jnp.where(mask_full, jnp.exp(step_scores - overall[..., None]), 0.0)
    numerator = pool_scale[..., None] * own_sum + jnp.einsum(
        "bskgj,bjkd->bskgd", step_weights, value_heads, precision=lax.Precision.HIGHEST
    )
    denominator = pool_scale * own_total + jnp.sum(step_weights, axis=-1)
    result = numerator / denominator[..., None]
    return result.reshape(seq_count, STEPS, QH * HD).astype(jnp.bfloat16)


def prefill_part(prompt_queries, prompt_keys, prompt_values, prompt_positions):
    row_count = prompt_queries.shape[0]
    group_size = QH // KVH
    score_scale = HD ** (-0.5)
    query_heads = prompt_queries.reshape(row_count, KVH, group_size, HD)
    key_piece = lax.all_gather(prompt_keys, "seq", axis=0, tiled=True)
    value_piece = lax.all_gather(prompt_values, "seq", axis=0, tiled=True)
    position_piece = lax.all_gather(prompt_positions, "seq", axis=0, tiled=True)
    allowed = position_piece[None, :] <= prompt_positions[:, None]
    running_max = jnp.full((KVH, group_size, row_count), NEG_FILL, jnp.float32)
    key_heads = key_piece.reshape(-1, KVH, HD)
    scores = (
        jnp.einsum("rkgd,skd->kgrs", query_heads, key_heads, preferred_element_type=jnp.float32)
        * score_scale
    )
    scores = jnp.where(allowed[None, None], scores, NEG_FILL)
    new_max = jnp.maximum(running_max, jnp.max(scores, axis=-1))
    weights = jnp.where(allowed[None, None], jnp.exp(scores - new_max[..., None]), 0.0)
    value_heads = value_piece.reshape(-1, KVH, HD)
    mixed = jnp.einsum(
        "kgrs,skd->rkgd",
        weights.astype(jnp.bfloat16),
        value_heads,
        preferred_element_type=jnp.float32,
    )
    new_total = jnp.sum(weights, axis=-1)
    ratio = mixed / jnp.transpose(new_total, (2, 0, 1))[..., None]
    return ratio.reshape(row_count, QH * HD).astype(jnp.bfloat16)


def decode_part(
    step_queries, step_keys, step_values, pool_keys, pool_values, page_owner, page_fill
):
    seq_dev = step_queries.shape[0]
    total_seqs = lax.axis_size("seq") * seq_dev
    group_size = QH // KVH
    page_count = pool_keys.shape[0]
    every_query = lax.all_gather(step_queries, "seq", axis=0, tiled=True)
    owner = page_owner[:, 0]
    page_queries = jnp.take(every_query, owner, axis=0).reshape(
        page_count, STEPS, KVH, group_size, HD
    )
    key_heads = pool_keys.reshape(page_count, PAGE, KVH, HD)
    value_heads = pool_values.reshape(page_count, PAGE, KVH, HD)
    scores = jnp.einsum(
        "pskgd,pjkd->pskgj", page_queries, key_heads, preferred_element_type=jnp.float32
    ) * HD ** (-0.5)
    valid = jnp.arange(PAGE)[None, :] < page_fill[:, None]
    valid_full = valid[:, None, None, None, :]
    scores = jnp.where(valid_full, scores, NEG_FILL)
    page_max = jnp.max(scores, axis=-1)
    member = owner[None, :] == jnp.arange(total_seqs, dtype=jnp.int32)[:, None]
    local_max = jnp.max(jnp.where(member[:, :, None, None, None], page_max[None], NEG_FILL), axis=1)
    pool_max = lax.pmax(local_max.astype(jnp.bfloat16), "seq").astype(local_max.dtype)
    page_top = jnp.take(pool_max, owner, axis=0)
    pool_weight = jnp.where(valid_full, jnp.exp(scores - page_top[..., None]), 0.0).astype(
        jnp.bfloat16
    )
    page_sum = jnp.einsum(
        "pskgj,pjkd->pskgd", pool_weight, value_heads, preferred_element_type=jnp.float32
    )
    page_total = jnp.sum(pool_weight.astype(jnp.float32), axis=-1)
    member_matrix = member.astype(jnp.float32)
    seq_sum = jnp.dot(
        member_matrix, page_sum.reshape(page_count, -1), precision=lax.Precision.HIGHEST
    )
    seq_total = jnp.dot(
        member_matrix, page_total.reshape(page_count, -1), precision=lax.Precision.HIGHEST
    )
    own_start = lax.axis_index("seq") * seq_dev
    own_max = lax.dynamic_slice_in_dim(pool_max, own_start, seq_dev, 0)
    whole_sum, whole_total = lax.psum((seq_sum, seq_total), "seq")
    own_sum = lax.dynamic_slice_in_dim(whole_sum, own_start, seq_dev, 0)
    own_total = lax.dynamic_slice_in_dim(whole_total, own_start, seq_dev, 0)
    own_sum = own_sum.reshape(seq_dev, STEPS, KVH, group_size, HD)
    own_total = own_total.reshape(seq_dev, STEPS, KVH, group_size)
    return finish_steps(step_queries, step_keys, step_values, own_max, own_sum, own_total)


def shards(
    prompt_queries,
    prompt_keys,
    prompt_values,
    prompt_positions,
    step_queries,
    step_keys,
    step_values,
    pool_keys,
    pool_values,
    page_owner,
    page_fill,
):
    prefill_out = prefill_part(prompt_queries, prompt_keys, prompt_values, prompt_positions)
    decode_out = decode_part(
        step_queries, step_keys, step_values, pool_keys, pool_values, page_owner, page_fill
    )
    return (prefill_out, decode_out)


def solution(mesh):
    in_specs = (
        P(("group", "seq"), None),
        P(("group", "seq"), None),
        P(("group", "seq"), None),
        P(("group", "seq")),
        P(("group", "seq"), None, None),
        P(("group", "seq"), None, None),
        P(("group", "seq"), None, None),
        P(("group", "seq"), None, None),
        P(("group", "seq"), None, None),
        P(("group", "seq"), None),
        P(("group", "seq")),
    )
    out_specs = (P(("group", "seq"), None), P(("group", "seq"), None, None))
    return jax.shard_map(shards, mesh=mesh, in_specs=in_specs, out_specs=out_specs, check_vma=False)
```

profile of v0, /device:TPU:1, one launch (start us, length us, event | category | flops | bytes accessed | tf_op | source)
XLA Modules:
  0.0 300.4 jit_solution(10491668119817431259)
XLA Ops:
  7.2 0.0 copy-start
  7.2 0.0 all-reduce.3.cloned.1.call-start
  7.2 0.7 fusion.53
  7.9 0.7 and_bitcast_fusion
  8.5 0.7 iota_compare_fusion
  9.3 23.9 %all_gather.15 = bf16[16,2,4096]{2,1,0:T(2,128)(2,1)S(1)} all-gather(bf16[1,2,4096]{2,1,0:T(2,128)(2,1)} %param.15), channel_id=1, replica_groups=mesh['group'=2,'seq'=16] {'seq'}, dimensions={0}, use_global_device_ids=true | all-gather | bytes 278528 | tf_op jit(solution)/shard_map/all_gather | solution.py:76
  33.2 0.0 copy-start.4
  33.2 1.6 gather_fusion
  34.8 0.4 gather.11
  35.2 6.9 %reshape.187 = bf16[32,128,4,128]{3,2,1,0:T(4,128)(2,1)} reshape(bf16[32,128,512]{2,1,0:T(8,128)(2,1)} %param.18) | data formatting | bytes 8388608 | tf_op jit(solution)/shard_map/reshape | solution.py:81
  42.1 4.7 %fusion.57 = (bf16[32,2,4,8]{3,1,2,0:T(2,128)(2,1)S(1)}, f32[32,2,4,8,128]{4,3,1,2,0:T(8,128)S(1)}) fusion(bf16[32,128,4,128,1]{3,2,1,0,4:T(4,128)(2,1)} %bitcast.130, bf16[32,2,4,8,128]{4,3,2,1,0:T(8,128)(2,1)S(1)} %gather.11, pred[32]{0:T(512)(128)(4,1)S(1)} %and_bitcast_fusion, pred[32,128]{1,0:T(8,128)(4,1)S(1)} %iota_compare_fusion), kind=kOutput, calls=%fused_computation.74 | convolution fusion | flops 68155392 | bytes 5775392 | tf_op jit(solution)/shard_map/pskgd,pjkd->pskgj/dot_general | solution.py:83
  46.8 0.1 copy.83
  46.9 0.0 copy-done.4
  46.9 0.3 select_reduce_fusion
  47.2 53.0 %pmax.7 = bf16[16,2,4,8]{3,2,1,0:T(4,128)(2,1)S(1)} all-reduce(bf16[16,2,4,8]{3,2,1,0:T(4,128)(2,1)S(1)} %select_reduce_fusion), channel_id=1, replica_groups=mesh['group'=2,'seq'=16] {'seq'}, use_global_device_ids=true, to_apply=%region_4.5 | all-reduce | flops 1024 | bytes 4096 | tf_op jit(solution)/shard_map/pmax | solution.py:92
  100.2 0.6 gather_fusion.1
  100.8 0.1 broadcast_select_fusion
  100.9 0.1 copy.89
  101.0 6.9 %reshape.190 = bf16[32,128,4,128]{3,2,1,0:T(4,128)(2,1)} reshape(bf16[32,128,512]{2,1,0:T(8,128)(2,1)} %param.19) | data formatting | bytes 8388608 | tf_op jit(solution)/shard_map/reshape | solution.py:82
  108.0 0.0 copy-start.3
  108.0 0.0 copy-start.6
  108.0 0.0 copy-start.7
  108.0 0.0 copy-start.2
  108.0 3.5 %fusion.22 = f32[32,2,4,8,128]{4,3,1,2,0:T(8,128)S(1)} fusion(bf16[32,128,4,128,1]{3,2,1,0,4:T(4,128)(2,1)} %bitcast.131, f32[32,2,4,8,128]{4,3,1,2,0:T(8,128)S(1)} %get-tuple-element.9, f32[32,2,4,8]{3,1,2,0:T(2,128)S(1)} %copy.89, pred[32,128]{1,0:T(8,128)(4,1)S(1)} %iota_compare_fusion), kind=kOutput, calls=%fused_computation.17 | convolution fusion | flops 67895296 | bytes 6303744 | tf_op jit(solution)/shard_map/pskgj,pjkd->pskgd/dot_general | solution.py:97
  111.5 0.1 copy.91
  111.6 1.9 fusion.28
  113.5 0.0 all-reduce.3.cloned.1.call-update
  113.5 0.0 all-gather.3.cloned.1.call-start
  113.6 0.7 all-gather.3.cloned.1.call-update
  114.3 0.0 all-gather.5.cloned.1.call-start
  114.3 0.7 all-gather.5.cloned.1.call-update
  115.0 0.8 convert_reduce_fusion
  115.8 0.1 copy.97
  115.9 0.1 fusion.40
  116.1 34.6 %psum.15 = f32[16,64]{1,0:T(8,128)S(1)} all-reduce(f32[16,64]{1,0:T(8,128)S(1)} %fusion.40), channel_id=1, replica_groups=mesh['group'=2,'seq'=16] {'seq'}, use_global_device_ids=true, to_apply=%region_8.9 | all-reduce | flops 1024 | bytes 8192 | tf_op jit(solution)/shard_map/psum | solution.py:110
  150.7 0.1 reshape.196
  150.8 0.0 copy-done.3
  150.8 0.0 copy-done.6
  150.8 0.2 convolution_multiply_fusion
  150.9 0.1 fusion.39
  151.1 0.1 fusion.56
  151.2 0.0 copy-done.7
  151.2 0.6 dynamic-slice
  152.5 0.0 copy-done.5
  152.5 0.2 dynamic-update-slice
  152.7 5.5 %all-reduce = s32[1024]{0:T(1024)S(1)} all-reduce(s32[1024]{0:T(1024)S(1)} %dynamic-update-slice), channel_id=1, replica_groups=mesh['group'=2,'seq'=16] {'seq'}, use_global_device_ids=true, to_apply=%add | all-reduce | flops 1024 | bytes 8192
  158.2 0.1 broadcast_compare_fusion
  158.3 0.0 copy-done.2
  158.3 0.1 copy.117
  158.4 47.7 %all-reduce.3.cloned.1.call-done = f32[16,8192]{1,0:T(8,128)} async-done(((f32[16,8192]{1,0:T(8,128)}), f32[16,8192]{1,0:T(8,128)}) %all-reduce.3.cloned.1.call-update) | async-done | bytes 524304 | tf_op jit(solution)/shard_map/psum | solution.py:110
  206.1 1.0 constant_dynamic-slice_fusion.1
  207.1 0.0 copy-done
  207.1 0.2 fusion.27
  207.3 0.6 convert_element_type.45
  208.0 38.6 %all-gather.3.cloned.1.call-done = bf16[1024,512]{1,0:T(8,128)(2,1)} async-done(((bf16[64,512]{1,0:T(8,128)(2,1)}), bf16[1024,512]{1,0:T(8,128)(2,1)}) %all-gather.3.cloned.1.call-update) | async-done | bytes 1048592 | tf_op jit(solution)/shard_map/all_gather | solution.py:44
  246.6 1.5 copy.75
  248.0 1.7 fusion
  249.8 3.2 %copy-done.1 = f32[4,1024,64,8]{1,2,3,0:T(8,128)} copy-done((f32[4,1024,64,8]{1,2,3,0:T(8,128)}, f32[4,1024,64,8]{1,2,3,0:T(8,128)S(1)}, u32[]{:S(2)}) %copy-start.1) | copy-done | bytes 8388632
  253.0 2.7 fusion.1
  255.6 30.0 %all-gather.5.cloned.1.call-done = bf16[1024,512]{1,0:T(8,128)(2,1)} async-done(((bf16[64,512]{1,0:T(8,128)(2,1)}), bf16[1024,512]{1,0:T(8,128)(2,1)}) %all-gather.5.cloned.1.call-update) | async-done | bytes 1048592 | tf_op jit(solution)/shard_map/all_gather | solution.py:45
  285.6 1.5 copy.78
  287.1 5.4 %divide_convert_fusion = bf16[64,4,8,128]{3,0,2,1:T(8,128)(2,1)S(1)} fusion(bf16[1024,4,128,1]{0,2,3,1:T(8,128)(2,1)S(1)} %bitcast.135, f32[4,1024,64,8]{1,2,3,0:T(8,128)} %copy-done.1, f32[4,8,64]{2,1,0:T(8,128)S(1)} %broadcast_maximum_fusion, pred[64,1024]{1,0:T(8,128)(4,1)S(1)} %broadcast_compare_fusion, f32[64,4,8]{0,2,1:T(8,128)S(1)} %bitcast.140), kind=kOutput, calls=%fused_computation.28 | convolution fusion | flops 547880960 | bytes 10043392 | tf_op jit(solution)/shard_map/kgrs,skd->rkgd/dot_general | solution.py:58
  292.5 0.3 copy.80
  292.8 1.0 copy.177
  (15 shorter events, 0.1 us)
Async XLA Ops:
  7.2 199.9 %copy-start = (bf16[1,2,512]{2,1,0:T(2,128)(2,1)S(1)}, bf16[1,2,512]{2,1,0:T(2,128)(2,1)}, u32[]{:S(2)}) copy-start(bf16[1,2,512]{2,1,0:T(2,128)(2,1)} %param.17) | copy-start | bytes 6148
  7.2 198.9 %all-reduce.3.cloned.1.call-start = ((), (), s32[]{:S(2)}) async-start(), calls=%async_computation.2 | async-start | bytes 1048576 | tf_op jit(solution)/shard_map/psum | solution.py:110
  33.2 13.7 %copy-start.4 = (s32[32,1]{0,1:T(1,128)S(1)}, s32[32,1]{0,1:T(1,128)}, u32[]{:S(2)}) copy-start(s32[32,1]{0,1:T(1,128)} %param.20) | copy-start | bytes 388
  108.0 42.8 %copy-start.3 = (bf16[1,2,4096]{2,1,0:T(2,128)(2,1)S(1)}, bf16[1,2,4096]{2,1,0:T(2,128)(2,1)}, u32[]{:S(2)}) copy-start(bf16[1,2,4096]{2,1,0:T(2,128)(2,1)} %param.15) | copy-start | bytes 49156
  108.0 42.8 %copy-start.6 = (bf16[1,2,512]{2,1,0:T(2,128)(2,1)S(1)}, bf16[1,2,512]{2,1,0:T(2,128)(2,1)}, u32[]{:S(2)}) copy-start(bf16[1,2,512]{2,1,0:T(2,128)(2,1)} %param.16) | copy-start | bytes 6148
  108.0 43.3 %copy-start.7 = (u32[32]{0:T(128)S(1)}, u32[32]{0:T(128)}, u32[]{:S(2)}) copy-start(u32[32]{0:T(128)} %constant.51) | copy-start | bytes 388
  108.0 44.5 %copy-start.5 = (s32[64]{0:T(128)S(1)}, s32[64]{0:T(128)}, u32[]{:S(2)}) copy-start(s32[64]{0:T(128)} %param.14) | copy-start | bytes 772
  108.0 50.4 %copy-start.2 = (bf16[64,4096]{1,0:T(8,128)(2,1)S(1)}, bf16[64,4096]{1,0:T(8,128)(2,1)}, u32[]{:S(2)}) copy-start(bf16[64,4096]{1,0:T(8,128)(2,1)} %param.11) | copy-start | bytes 1572868
  113.5 133.0 %all-gather.3.cloned.1.call-start = ((), (), s32[]{:S(2)}) async-start(), calls=%async_computation | async-start | bytes 1114112 | tf_op jit(solution)/shard_map/all_gather | solution.py:44
  114.3 171.3 %all-gather.5.cloned.1.call-start = ((), (), s32[]{:S(2)}) async-start(), calls=%async_computation.1 | async-start | bytes 1114112 | tf_op jit(solution)/shard_map/all_gather | solution.py:45
  249.7 3.2 %copy-start.1 = (f32[4,1024,64,8]{1,2,3,0:T(8,128)}, f32[4,1024,64,8]{1,2,3,0:T(8,128)S(1)}, u32[]{:S(2)}) copy-start(f32[4,1024,64,8]{1,2,3,0:T(8,128)S(1)} %get-tuple-element.7) | copy-start | bytes 25165828
Sparse Core Ops, SparseCore 0:
  113.7 92.4 all-reduce.2
  208.3 38.2 all-gather.2
  248.7 36.8 all-gather.4
where the time goes:
time: 301 us; the launch traced here: 300 us
  waiting for transfers between devices  118 us (39%)
  blocking collectives  117 us (39%)
  local copies, waits for them, and re-layouts  27.1 us (9%)
  matrix products  17.6 us (6%)
  between operations  14.7 us (5%)
  other arithmetic  6.23 us (2%)
    pmax x1, blocking collectives, decode_part(): lax.pmax(local_max.astype(jnp.bfloat16), 'seq').astype(local_max.dtype)  53 us
    psum x1, waiting for transfers between devices, decode_part(): whole_sum, whole_total = lax.psum((seq_sum, seq_total), 'seq')  47.7 us
    all_gather x1, waiting for transfers between devices, prefill_part(): key_piece = lax.all_gather(prompt_keys, 'seq', axis=0, tiled=True)  38.6 us
    psum x1, blocking collectives, decode_part(): whole_sum, whole_total = lax.psum((seq_sum, seq_total), 'seq')  34.6 us
    all_gather x1, waiting for transfers between devices, prefill_part(): value_piece = lax.all_gather(prompt_values, 'seq', axis=0, tiled=True)  30 us
    all_gather x1, blocking collectives, decode_part(): every_query = lax.all_gather(step_queries, 'seq', axis=0, tiled=True)  23.9 us
    reshape x1, local copies, waits for them, and re-layouts, decode_part(): value_heads = pool_values.reshape(page_count, PAGE, KVH, HD)  6.93 us
    reshape x1, local copies, waits for them, and re-layouts, decode_part(): key_heads = pool_keys.reshape(page_count, PAGE, KVH, HD)  6.93 us
  transfers between devices with their start and end apart: 3, of which 3 were waited for; matrix products, arithmetic and copies ran while one was open for 3% of the time, Pallas kernels for 0%

commit v1 on v0

v1 whole, which is shorter than its diff:
```python
import functools
import jax
import jax.numpy as jnp
from jax import lax
from jax.experimental import pallas as pl
from jax.experimental.pallas import tpu as pltpu
from jax.sharding import PartitionSpec as P

QH = 32
KVH = 4
HD = 128
GROUP = QH // KVH
PAGE = 128
STEPS = 2
ROWS = STEPS * QH
HEAD_ROWS = STEPS * GROUP
MSG = ROWS + 16
SEQ_BLOCK = 16
NEG = -1e30
LOG2E = 1.4426950408889634
SCALE = HD ** (-0.5) * LOG2E
MESH = pl.DeviceIdType.MESH
NT = (((1,), (1,)), ((), ()))


def kernel(
    n,
    X,
    qmsg,
    row_pos,
    tok_owner,
    pq,
    own_k,
    own_v,
    step_k,
    step_v,
    pool_k_hbm,
    pool_v_hbm,
    out,
    dec,
    qall,
    kv,
    pool_k,
    pool_v,
    key_pos,
    psend,
    precv,
    stats,
    stats_in,
    pool_sem,
    q_send,
    q_sib,
    q_recv,
    p_send,
    p_recv,
    up_send,
    down_send,
    x_send,
    sib_send,
    kv_recv,
):
    Z = n // (2 * X)
    half = n // 2
    me = lax.axis_index("seq")
    c = lax.rem(me, 2)
    x = lax.rem(me // 2, X)
    z = me // (2 * X)
    sib = me + 1 - 2 * c
    tok = own_k.shape[0]
    keys = n * tok
    tokens = pool_k.shape[0]

    pool_copies = [
        pltpu.make_async_copy(pool_k_hbm, pool_k, pool_sem.at[0]),
        pltpu.make_async_copy(pool_v_hbm, pool_v, pool_sem.at[1]),
    ]
    barrier = pltpu.get_barrier_semaphore()

    def greet(i, carry):
        pl.semaphore_signal(
            barrier, inc=1, device_id={"seq": lax.rem(me + i, n)}, device_id_type=MESH
        )
        return carry

    lax.fori_loop(1, n, greet, 0)
    for copy in pool_copies:
        copy.start()
    qall[me] = qmsg[...]
    kv[me, :, : KVH * HD] = own_k[...]
    kv[me, :, KVH * HD :] = own_v[...]
    stats[...] = jnp.full_like(stats, NEG)
    stats_in[...] = jnp.full_like(stats_in, NEG)
    pl.semaphore_wait(barrier, n - 1)

    def remote(buf, b, peer, ss, rs):
        return pltpu.make_async_remote_copy(
            src_ref=buf.at[b],
            dst_ref=buf.at[b],
            send_sem=ss,
            recv_sem=rs.at[b],
            device_id={"seq": peer},
            device_id_type=MESH,
        )

    def q_copy(j):
        return remote(qall, me, lax.rem(me + 2 * j, n), q_send.at[j], q_recv)

    def q_fwd(j):
        b = lax.rem(me + 2 * j, n)
        return remote(qall, b, sib, q_sib.at[j], q_recv)

    def loop(lo, hi, body):
        def step(i, carry):
            body(i)
            return carry

        lax.fori_loop(lo, hi, step, 0)

    loop(1, half, lambda j: q_copy(j).start())
    q_fwd(0).start()

    def to_up(b, zb):
        return remote(kv, b, me + 2 * X, up_send.at[zb], kv_recv)

    def to_down(b, zb):
        return remote(kv, b, me - 2 * X, down_send.at[zb], kv_recv)

    def to_x(b, zb, i):
        peer = z * 2 * X + lax.rem(x + i, X) * 2 + c
        return remote(kv, b, peer, x_send.at[zb * X + i], kv_recv)

    def to_sib(b):
        return remote(kv, b, sib, sib_send.at[b // 2], kv_recv)

    def arrived(b):
        remote(kv, b, sib, sib_send.at[0], kv_recv).wait_recv()

    def column(zb):
        return zb * 2 * X + x * 2 + c

    for i in range(1, X):
        to_x(me, z, i).start()

    @pl.when(z + 1 < Z)
    def _():
        to_up(me, z).start()

    @pl.when(z >= 1)
    def _():
        to_down(me, z).start()

    to_sib(me).start()

    def both(*conditions):
        bits = [jnp.where(one, 1, 0) for one in conditions]
        return functools.reduce(lambda p, q: p * q, bits) == 1

    def along_z(h, here):
        below, above = column(z - h), column(z + h)

        @pl.when(both(here, z >= h))
        def _():
            arrived(below)
            for i in range(1, X):
                to_x(below, z - h, i).start()
            to_sib(below).start()

        @pl.when(both(here, z >= h, z + 1 < Z))
        def _():
            to_up(below, z - h).start()

        @pl.when(both(here, z + h < Z))
        def _():
            arrived(above)
            for i in range(1, X):
                to_x(above, z + h, i).start()
            to_sib(above).start()

        @pl.when(both(here, z + h < Z, z >= 1))
        def _():
            to_down(above, z + h).start()

    def pass_on(zb):
        for i in range(1, X):
            b = zb * 2 * X + lax.rem(x + i, X) * 2 + c
            arrived(b)
            to_sib(b).start()

    def across_x(h, here):
        @pl.when(both(here, z >= h))
        def _():
            pass_on(z - h)

        if h > 0:

            @pl.when(both(here, z + h < Z))
            def _():
                pass_on(z + h)

    def q_take(j):
        b = lax.rem(me + 2 * j, n)
        remote(qall, b, sib, q_sib.at[0], q_recv).wait_recv()
        q_fwd(j).start()

    loop(1, half, q_take)

    def q_other(j):
        b = lax.rem(sib + 2 * j, n)
        remote(qall, b, sib, q_sib.at[0], q_recv).wait_recv()

    loop(0, half, q_other)

    lane = lax.broadcasted_iota(jnp.int32, (1, 2 * tok), 1)
    for i in range(half):
        pair = []
        for b in (2 * i, 2 * i + 1):
            coded = qall[b, ROWS:MSG, :].astype(jnp.float32)
            pair.append(coded[0:1] * 128.0 + coded[1:2])
        key_pos[:, i * 2 * tok : (i + 1) * 2 * tok] = jnp.where(lane < tok, pair[0], pair[1])

    for copy in pool_copies:
        copy.wait()

    def attend(q, count, load):
        rows = q.shape[0]

        def chunk(t, carry):
            m, l, acc = carry
            k, v, allowed = load(t)
            s = lax.dot_general(q, k, NT, preferred_element_type=jnp.float32) * SCALE
            s = jnp.where(allowed, s, NEG)
            new = jnp.maximum(m, jnp.max(s, axis=1, keepdims=True))
            w = jnp.exp2(s - new)
            scale = jnp.exp2(m - new)
            l = l * scale + jnp.sum(w, axis=1, keepdims=True)
            acc = acc * scale + jnp.dot(
                w.astype(jnp.bfloat16), v, preferred_element_type=jnp.float32
            )
            return new, l, acc

        carry = (
            jnp.full((rows, 1), NEG, jnp.float32),
            jnp.zeros((rows, 1), jnp.float32),
            jnp.zeros((rows, HD), jnp.float32),
        )
        if count == 1:
            return chunk(0, carry)
        return lax.fori_loop(0, count, chunk, carry)

    chunk_tok = 1024
    drows = SEQ_BLOCK * HEAD_ROWS
    row_seq = lax.broadcasted_iota(jnp.int32, (drows, 1), 0) // HEAD_ROWS
    lane16 = lax.broadcasted_iota(jnp.int32, (HEAD_ROWS, 128), 1)

    def decode_head(h):
        for k in range(1, min(Z, KVH)):
            along_z(k, h == k)
            across_x(k - 1, h == k)

        hrow = pl.multiple_of(h * HEAD_ROWS, HEAD_ROWS)
        hlane = pl.ds(pl.multiple_of(h * HD, HD), HD)

        def seq_block(sb):
            first = sb * SEQ_BLOCK
            q = qall[pl.ds(first, SEQ_BLOCK), pl.ds(hrow, HEAD_ROWS), :].reshape(drows, HD)

            def load(t):
                at = pl.ds(pl.multiple_of(t * chunk_tok, chunk_tok), chunk_tok)
                return pool_k[at, hlane], pool_v[at, hlane], tok_owner[:, at] == row_seq + first

            m, l, acc = attend(q, tokens // chunk_tok, load)
            o = (acc / l).astype(jnp.bfloat16).reshape(SEQ_BLOCK, HEAD_ROWS, HD)
            psend[pl.ds(first, SEQ_BLOCK), pl.ds(hrow, HEAD_ROWS), :] = o
            lse = m + jnp.log2(l)
            seen = stats[pl.ds(hrow, HEAD_ROWS), :]
            for i in range(SEQ_BLOCK):
                seen = jnp.where(
                    lane16 == first + i, lse[i * HEAD_ROWS : (i + 1) * HEAD_ROWS], seen
                )
            stats[pl.ds(hrow, HEAD_ROWS), :] = seen

        loop(0, n // SEQ_BLOCK, seq_block)

    loop(0, KVH, decode_head)

    stats[...] = jnp.transpose(stats[...])
    sub16 = lax.broadcasted_iota(jnp.int32, (16, 128), 0)

    def code(b):
        row = jnp.broadcast_to(stats[pl.ds(b, 1), :], (16, 128))
        hi = row.astype(jnp.bfloat16).astype(jnp.float32)
        mid = (row - hi).astype(jnp.bfloat16).astype(jnp.float32)
        low = row - hi - mid
        coded = jnp.where(sub16 == 0, hi, jnp.where(sub16 == 1, mid, low))
        psend[b, ROWS:MSG, :] = coded.astype(jnp.bfloat16)

    loop(0, n, code)

    def p_copy(j):
        b = lax.rem(me + j, n)
        return pltpu.make_async_remote_copy(
            src_ref=psend.at[b],
            dst_ref=precv.at[me],
            send_sem=p_send.at[j],
            recv_sem=p_recv.at[me],
            device_id={"seq": b},
            device_id_type=MESH,
        )

    loop(1, n, lambda j: p_copy(j).start())
    precv[me] = psend[me]

    for h in range(min(Z, KVH), Z):
        along_z(h, True)
        across_x(h - 1, True)
    across_x(Z - 1, True)

    def kv_other(j):
        arrived(2 * j + 1 - c)

    loop(0, half, kv_other)

    part = 4
    pos_col = jnp.concatenate([row_pos[:, 0:1]] * part, axis=0)
    chunk_keys = 1024
    blocks = chunk_keys // tok

    def prefill(u):
        h = u // (GROUP // part)
        q = jnp.concatenate(
            [
                pq[:, pl.ds(pl.multiple_of((u * part + g) * HD, HD), HD)]
                for g in range(part)
            ],
            axis=0,
        )

        def load(t):
            at = pl.ds(t * blocks, blocks)
            k = kv[at, :, pl.ds(pl.multiple_of(h * HD, HD), HD)].reshape(chunk_keys, HD)
            v = kv[at, :, pl.ds(pl.multiple_of((KVH + h) * HD, HD), HD)].reshape(chunk_keys, HD)
            pos = key_pos[:, pl.ds(pl.multiple_of(t * chunk_keys, chunk_keys), chunk_keys)]
            return k, v, pos <= pos_col

        m, l, acc = attend(q, keys // chunk_keys, load)
        o = (acc / l).astype(jnp.bfloat16)
        for g in range(part):
            out[:, pl.ds(pl.multiple_of((u * part + g) * HD, HD), HD)] = o[g * tok : (g + 1) * tok]

    loop(0, QH // part, prefill)

    def p_take(j):
        b = lax.rem(me + j, n)
        pltpu.make_async_remote_copy(
            src_ref=psend.at[b],
            dst_ref=precv.at[b],
            send_sem=p_send.at[0],
            recv_sem=p_recv.at[b],
            device_id={"seq": b},
            device_id_type=MESH,
        ).wait_recv()

    loop(1, n, p_take)

    def decode_stat(d):
        coded = precv[d, ROWS:MSG, :].astype(jnp.float32)
        stats_in[pl.ds(d, 1), :] = coded[0:1] + coded[1:2] + coded[2:3]

    loop(0, n, decode_stat)
    lse = jnp.transpose(stats_in[...])[0:ROWS]
    q = qmsg[0:ROWS, :].astype(jnp.float32)
    row_id = lax.broadcasted_iota(jnp.int32, (ROWS, 1), 0)
    row_step = (row_id // GROUP) % STEPS
    scores = []
    for j in range(STEPS):
        s = jnp.sum(q * step_k[j], axis=1, keepdims=True) * SCALE
        scores.append(jnp.where(row_step >= j, s, NEG))
    top = jnp.max(lse, axis=1, keepdims=True)
    for s in scores:
        top = jnp.maximum(top, s)
    w = jnp.exp2(lse - top)
    denominator = jnp.sum(w, axis=1, keepdims=True)
    numerator = jnp.zeros((ROWS, HD), jnp.float32)
    for j in range(STEPS):
        e = jnp.exp2(scores[j] - top)
        denominator += e
        numerator += e * step_v[j]
    dev = lax.broadcasted_iota(jnp.int32, (ROWS, 128), 1)

    def add(d, total):
        wd = jnp.sum(jnp.where(dev == d, w, 0.0), axis=1, keepdims=True)
        return total + wd * precv[d, 0:ROWS, :].astype(jnp.float32)

    numerator = lax.fori_loop(0, n, add, numerator, unroll=4)
    dec[...] = (numerator / denominator).astype(jnp.bfloat16)

    loop(1, half, lambda j: q_copy(j).wait_send())
    loop(0, half, lambda j: q_fwd(j).wait_send())
    loop(1, n, lambda j: p_copy(j).wait_send())
    for h in range(Z):

        @pl.when(both(z >= h, z + 1 < Z))
        def _():
            to_up(column(z - h), z - h).wait_send()

        @pl.when(both(z + h < Z, z >= 1))
        def _():
            to_down(column(z + h), z + h).wait_send()

    def left(zb):
        for i in range(1, X):
            to_x(column(zb), zb, i).wait_send()

    loop(0, Z, left)
    loop(0, half, lambda j: to_sib(2 * j + c).wait_send())


def shards(
    prompt_queries,
    prompt_keys,
    prompt_values,
    prompt_positions,
    step_queries,
    step_keys,
    step_values,
    pool_keys,
    pool_values,
    page_owner,
    page_fill,
):
    n = lax.axis_size("seq")
    X = max(1, round((n // 2) ** (1 / 3)))
    Z = n // (2 * X)
    tok = prompt_queries.shape[0]
    pages = pool_keys.shape[0]
    tokens = pages * PAGE
    rows = jnp.transpose(
        step_queries.reshape(STEPS, KVH, GROUP, HD), (1, 0, 2, 3)
    ).reshape(ROWS, HD)
    twice = jnp.concatenate([prompt_positions, prompt_positions])[None]
    coded = jnp.concatenate([twice // 128, twice % 128, jnp.zeros((14, 2 * tok), jnp.int32)])
    qmsg = jnp.concatenate([rows, coded.astype(jnp.bfloat16)])
    row_pos = jnp.broadcast_to(prompt_positions.astype(jnp.float32)[:, None], (tok, 128))
    valid = jnp.arange(PAGE)[None, :] < page_fill[:, None]
    tok_owner = jnp.where(valid, page_owner, -1).reshape(1, tokens)

    def per_row(a):
        a = a.astype(jnp.float32).reshape(STEPS, KVH, 1, HD)
        return jnp.broadcast_to(a, (STEPS, KVH, HEAD_ROWS, HD)).reshape(STEPS, ROWS, HD)

    vmem = pl.BlockSpec(memory_space=pltpu.VMEM)
    hbm = pl.BlockSpec(memory_space=pl.ANY)
    dma = pltpu.SemaphoreType.DMA
    bf16 = jnp.bfloat16
    prefill_out, dec = pl.pallas_call(
        functools.partial(kernel, n, X),
        out_shape=(
            jax.ShapeDtypeStruct((tok, QH * HD), bf16),
            jax.ShapeDtypeStruct((ROWS, HD), bf16),
        ),
        in_specs=[vmem] * 8 + [hbm] * 2,
        out_specs=(vmem, vmem),
        scratch_shapes=[
            pltpu.VMEM((n, MSG, HD), bf16),
            pltpu.VMEM((n, tok, 2 * KVH * HD), bf16),
            pltpu.VMEM((tokens, KVH * HD), bf16),
            pltpu.VMEM((tokens, KVH * HD), bf16),
            pltpu.VMEM((1, n * tok), jnp.float32),
            pltpu.VMEM((n, MSG, HD), bf16),
            pltpu.VMEM((n, MSG, HD), bf16),
            pltpu.VMEM((128, 128), jnp.float32),
            pltpu.VMEM((128, 128), jnp.float32),
            dma((2,)),
            dma((n // 2,)),
            dma((n // 2,)),
            dma((n,)),
            dma((n,)),
            dma((n,)),
            dma((Z,)),
            dma((Z,)),
            dma((Z * X,)),
            dma((n // 2,)),
            dma((n,)),
        ],
        compiler_params=pltpu.CompilerParams(
            collective_id=0, has_side_effects=True, vmem_limit_bytes=56 * 1024 * 1024
        ),
    )(
        qmsg,
        row_pos,
        tok_owner,
        prompt_queries,
        prompt_keys,
        prompt_values,
        per_row(step_keys),
        per_row(step_values),
        pool_keys.reshape(tokens, KVH * HD),
        pool_values.reshape(tokens, KVH * HD),
    )
    decode_out = jnp.transpose(dec.reshape(KVH, STEPS, GROUP, HD), (1, 0, 2, 3))
    return prefill_out, decode_out.reshape(1, STEPS, QH * HD)


def solution(mesh):
    rows = P(("group", "seq"), None)
    flat = P(("group", "seq"))
    cube = P(("group", "seq"), None, None)
    in_specs = (rows, rows, rows, flat, cube, cube, cube, cube, cube, rows, flat)
    return jax.shard_map(
        shards, mesh=mesh, in_specs=in_specs, out_specs=(rows, cube), check_vma=False
    )
```

time: 301 us -> 51.9 us (0.17)
  waiting for transfers between devices: 118 us -> 0 us
  blocking collectives: 117 us -> 0 us
  Pallas kernels: 0 us -> 40 us
  local copies, waits for them, and re-layouts: 27.1 us -> 7.33 us
  matrix products: 17.6 us -> 0 us
  between operations: 14.7 us -> 0.65 us
    all_gather x2 -> x0, waiting for transfers between devices: 68.6 us -> none  [the longest x1 38.6 us: prefill_part(): key_piece = lax.all_gather(prompt_keys, 'seq', axis=0, tiled=True)]
    pmax x1 -> x0, blocking collectives: 53 us -> none  [decode_part(): lax.pmax(local_max.astype(jnp.bfloat16), 'seq').astype(local_max.dtype)]
    psum x1 -> x0, waiting for transfers between devices: 47.7 us -> none  [decode_part(): whole_sum, whole_total = lax.psum((seq_sum, seq_total), 'seq')]
    pallas_call x0 -> x1, Pallas kernels: none -> 40 us  [shards(): pl.pallas_call(functools.partial(kernel, n, X), out_shape=(jax.ShapeDtype...]
    psum x1 -> x0, blocking collectives: 34.6 us -> none  [decode_part(): whole_sum, whole_total = lax.psum((seq_sum, seq_total), 'seq')]
    all_gather x1 -> x0, blocking collectives: 23.9 us -> none  [decode_part(): every_query = lax.all_gather(step_queries, 'seq', axis=0, tiled=True)]
    dot_general x8 -> x0, matrix products: 17.6 us -> none  [the longest x1 5.39 us: prefill_part(): jnp.einsum('kgrs,skd->rkgd', weights.astype(jnp.bfloat16), value_heads, p...]
    reshape x3 -> x2, local copies, waits for them, and re-layouts: 14 us -> 0.62 us  [the longest x1 0.62 us: shards(): return (prefill_out, decode_out.reshape(1, STEPS, QH * HD))]
  transfers between devices with their start and end apart: 3 -> 0, of which waited for: 3 -> 0; matrix products, arithmetic and copies ran while one was open for 3% -> 0% of each run, Pallas kernels for 0% -> 0%
where the time goes in v1:
time: 51.9 us; the launch traced here: 51.5 us
  Pallas kernels  40 us (77%)
  local copies, waits for them, and re-layouts  7.33 us (14%)
  other arithmetic  3.51 us (7%)
  between operations  0.65 us (1%)
    pallas_call x1, Pallas kernels, shards(): pl.pallas_call(functools.partial(kernel, n, X), out_shape=(jax.ShapeDtype...  40 us
    broadcast_in_dim x4, local copies, waits for them, and re-layouts, per_row(): jnp.broadcast_to(a, (STEPS, KVH, HEAD_ROWS, HD)).reshape(STEPS, ROWS, HD)  2.64 us
    unnamed x2, local copies, waits for them, and re-layouts  2.59 us
    select_n x1, other arithmetic, shards(): tok_owner = jnp.where(valid, page_owner, -1).reshape(1, tokens)  1.35 us

profile of v1, /device:TPU:1, one launch (start us, length us, event | category | flops | bytes accessed | tf_op | source)
XLA Modules:
  0.0 51.5 jit_solution(7720010199842123277)
XLA Ops:
  0.6 0.7 %convert_element_type.2 = f32[64]{0:T(128)S(1)} convert(s32[64]{0:T(128)} %param.14) | non-fusion elementwise | flops 64 | bytes 512 | tf_op jit(solution)/shard_map/convert_element_type | solution.py:443
  1.3 0.1 pad.3.clone
  1.4 0.8 %fusion.2 = (bf16[1,128]{1,0:T(2,128)(2,1)S(1)}, s32[1,128]{1,0:T(1,128)S(1)}) fusion(s32[1,64]{1,0:T(1,128)} %bitcast.31), kind=kLoop, calls=%fused_computation.11 | loop fusion | flops 2176 | bytes 1024 | tf_op jit(solution)/shard_map/convert.2
  2.2 0.7 %reshape.303 = f32[2,4,128]{2,1,0:T(4,128)S(1)} reshape(bf16[1,2,512]{2,1,0:T(2,128)(2,1)} %param.16) | data formatting | bytes 6144 | tf_op jit(solution)/shard_map/broadcast_in_dim | solution.py:449
  2.9 0.7 %reshape.304 = f32[2,4,128]{2,1,0:T(4,128)S(1)} reshape(bf16[1,2,512]{2,1,0:T(2,128)(2,1)} %param.17) | data formatting | bytes 6144 | tf_op jit(solution)/shard_map/broadcast_in_dim | solution.py:449
  3.6 0.7 %copy.17 = bf16[1,2,32,128]{3,2,1,0:T(8,128)(2,1)S(1)} copy(bf16[1,2,32,128]{3,1,2,0:T(2,128)(2,1)} %bitcast.28) | data formatting | bytes 32768
  4.3 0.7 %maximum_maximum_fusion.qmsg = bf16[80,128]{1,0:T(8,128)(2,1)} fusion(bf16[1,128]{1,0:T(2,128)(2,1)S(1)} %fusion.1, bf16[1,128]{1,0:T(2,128)(2,1)S(1)} %get-tuple-element.6, bf16[64,128]{1,0:T(8,128)(2,1)S(1)} %bitcast.26, bf16[80]{0:T(256)(128)(2,1)S(1)} %pad.3.clone), kind=kLoop, calls=%fused_computation | loop fusion | flops 81920 | bytes 37536 | tf_op jit(solution)/shard_map/concatenate | solution.py:442
  5.0 1.4 %fusion = s32[32,128]{1,0:T(8,128)} fusion(s32[32]{0:T(128)} %bitcast.30, s32[32]{0:T(128)} %param.21), kind=kLoop, calls=%fused_computation.3 | loop fusion | flops 8192 | bytes 16640 | tf_op jit(solution)/shard_map/jit(_where)/select_n | solution.py:445
  6.3 0.7 %broadcast_in_dim.47.row_pos = f32[64,128]{1,0:T(8,128)} broadcast(f32[64]{0:T(128)S(1)} %convert_element_type.2), dimensions={0} | broadcast | bytes 33024 | tf_op jit(solution)/shard_map/broadcast_in_dim | solution.py:443
  7.0 0.6 %broadcast_in_dim.56 = f32[2,4,16,128]{3,2,1,0:T(8,128)} broadcast(f32[2,4,128]{2,1,0:T(4,128)S(1)} %reshape.304), dimensions={0,1,3} | broadcast | bytes 69632 | tf_op jit(solution)/shard_map/broadcast_in_dim | solution.py:449
  7.6 0.6 %broadcast_in_dim.53 = f32[2,4,16,128]{3,2,1,0:T(8,128)} broadcast(f32[2,4,128]{2,1,0:T(4,128)S(1)} %reshape.303), dimensions={0,1,3} | broadcast | bytes 69632 | tf_op jit(solution)/shard_map/broadcast_in_dim | solution.py:449
  8.3 40.0 %shard_map.122 = (bf16[64,4096]{1,0:T(8,128)(2,1)}, bf16[64,128]{1,0:T(8,128)(2,1)}) custom-call(bf16[80,128]{1,0:T(8,128)(2,1)} %maximum_maximum_fusion.qmsg, f32[64,128]{1,0:T(8,128)} %broadcast_in_dim.47.row_pos, s32[1,4096]{1,0:T(1,128)} %bitcast.25, bf16[64,4096]{1,0:T(8,128)(2,1)} %pq.1, bf16[64,512]{1,0:T(8,128)(2,1)} %own_k.1, ...), custom_call_target="tpu_custom_call" | custom-call | tf_op jit(solution)/shard_map/pallas_call | solution.py:455
  48.3 0.7 %copy.14 = bf16[2,4,8,128]{3,2,1,0:T(8,128)(2,1)S(1)} copy(bf16[2,4,8,128]{3,2,0,1:T(8,128)(2,1)} %bitcast.29) | data formatting | bytes 32768 | tf_op jit(solution)/shard_map/transpose | solution.py:500
  49.0 0.6 %reshape.302 = bf16[1,2,4096]{2,1,0:T(2,128)(2,1)} reshape(bf16[2,4,8,128]{3,2,1,0:T(8,128)(2,1)S(1)} %copy.14) | data formatting | bytes 32768 | tf_op jit(solution)/shard_map/reshape | solution.py:501
  49.6 1.9 %copy.19 = bf16[64,4096]{1,0:T(8,128)(2,1)} copy(bf16[64,4096]{1,0:T(8,128)(2,1)} %get-tuple-element.10) | data formatting | bytes 1048576
  (3 shorter events, 0.0 us)

commit v2 on v1

v2 whole, which is shorter than its diff:
```python
import functools
import jax
import jax.numpy as jnp
from jax import lax
from jax.experimental import pallas as pl
from jax.experimental.pallas import tpu as pltpu
from jax.sharding import PartitionSpec as P

QH = 32
KVH = 4
HD = 128
GROUP = QH // KVH
PAGE = 128
STEPS = 2
ROWS = STEPS * QH
HEAD_ROWS = STEPS * GROUP
MSG = ROWS + 16
SEQ_BLOCK = 16
NEG = -1e30
LOG2E = 1.4426950408889634
SCALE = HD ** (-0.5) * LOG2E
MESH = pl.DeviceIdType.MESH
NT = (((1,), (1,)), ((), ()))


def kernel(
    n,
    X,
    positions,
    page_owner,
    page_fill,
    step_q,
    pq,
    own_k,
    own_v,
    step_k,
    step_v,
    pool_k_hbm,
    pool_v_hbm,
    out,
    dec,
    qall,
    all_k,
    all_v,
    pool_k,
    pool_v,
    key_pos,
    tok_owner,
    psend,
    precv,
    stats,
    stats_in,
    own_q,
    own_dec,
    run_max,
    run_sum,
    run_out,
    pool_sem,
    q_send,
    q_sib,
    q_recv,
    p_send,
    p_recv,
    up_send,
    down_send,
    x_send,
    sib_send,
    k_recv,
    v_recv,
):
    Z = n // (2 * X)
    half = n // 2
    me = lax.axis_index("seq")
    c = lax.rem(me, 2)
    x = lax.rem(me // 2, X)
    z = me // (2 * X)
    sib = me + 1 - 2 * c
    tok = own_k.shape[0]
    keys = n * tok
    tokens = pool_k.shape[0]

    pool_copies = [
        pltpu.make_async_copy(pool_k_hbm, pool_k, pool_sem.at[0]),
        pltpu.make_async_copy(pool_v_hbm, pool_v, pool_sem.at[1]),
    ]
    barrier = pltpu.get_barrier_semaphore()

    def greet(i, carry):
        pl.semaphore_signal(
            barrier, inc=1, device_id={"seq": lax.rem(me + i, n)}, device_id_type=MESH
        )
        return carry

    lax.fori_loop(1, n, greet, 0)
    for copy in pool_copies:
        copy.start()
    all_k[me] = own_k[...]
    all_v[me] = own_v[...]
    wide_q = step_q[0].astype(jnp.float32)
    for j in range(QH):
        for i in range(STEPS):
            r = (j // GROUP) * HEAD_ROWS + i * GROUP + j % GROUP
            own_q[r : r + 1, :] = wide_q[i : i + 1, j * HD : (j + 1) * HD]
    qall[me, 0:ROWS, :] = own_q[...].astype(jnp.bfloat16)

    def row_position(i):
        return jnp.where(i < tok // 2, positions[0] + i, positions[tok // 2] + i - tok // 2)

    sub16 = lax.broadcasted_iota(jnp.int32, (16, 128), 0)
    lane_pos = row_position(lax.broadcasted_iota(jnp.int32, (16, 128), 1) % tok)
    coded = jnp.where(sub16 == 0, lane_pos // 128, lane_pos % 128)
    qall[me, ROWS:MSG, :] = coded.astype(jnp.float32).astype(jnp.bfloat16)
    stats[...] = jnp.full_like(stats, NEG)
    stats_in[...] = jnp.full_like(stats_in, NEG)
    pl.semaphore_wait(barrier, n - 1)

    def remote(buf, b, peer, ss, rs):
        return pltpu.make_async_remote_copy(
            src_ref=buf.at[b],
            dst_ref=buf.at[b],
            send_sem=ss,
            recv_sem=rs.at[b],
            device_id={"seq": peer},
            device_id_type=MESH,
        )

    def q_copy(j):
        return remote(qall, me, lax.rem(me + 2 * j, n), q_send.at[j], q_recv)

    def q_fwd(j):
        b = lax.rem(me + 2 * j, n)
        return remote(qall, b, sib, q_sib.at[j], q_recv)

    def loop(lo, hi, body):
        def step(i, carry):
            body(i)
            return carry

        lax.fori_loop(lo, hi, step, 0)

    loop(1, half, lambda j: q_copy(j).start())
    q_fwd(0).start()

    parts = ((0, all_k, k_recv), (1, all_v, v_recv))

    def to_up(b, zb, part):
        i, buf, rs = part
        return remote(buf, b, me + 2 * X, up_send.at[2 * zb + i], rs)

    def to_down(b, zb, part):
        i, buf, rs = part
        return remote(buf, b, me - 2 * X, down_send.at[2 * zb + i], rs)

    def to_x(b, zb, j, part):
        i, buf, rs = part
        peer = z * 2 * X + lax.rem(x + j, X) * 2 + c
        return remote(buf, b, peer, x_send.at[(zb * X + j) * 2 + i], rs)

    def to_sib(b, part):
        i, buf, rs = part
        return remote(buf, b, sib, sib_send.at[b // 2 * 2 + i], rs)

    def arrived(b, part):
        i, buf, rs = part
        remote(buf, b, sib, sib_send.at[i], rs).wait_recv()

    def column(zb):
        return zb * 2 * X + x * 2 + c

    def both(*conditions):
        bits = [jnp.where(one, 1, 0) for one in conditions]
        return functools.reduce(lambda p, q: p * q, bits) == 1

    for part in parts:

        @pl.when(z + 1 < Z)
        def _():
            to_up(me, z, part).start()

        @pl.when(z >= 1)
        def _():
            to_down(me, z, part).start()

        for j in range(1, X):
            to_x(me, z, j, part).start()
        to_sib(me, part).start()

    def along_z(h, here):
        below, above = column(z - h), column(z + h)
        for part in parts:

            @pl.when(both(here, z >= h))
            def _():
                arrived(below, part)

            @pl.when(both(here, z >= h, z + 1 < Z))
            def _():
                to_up(below, z - h, part).start()

            @pl.when(both(here, z >= h))
            def _():
                for j in range(1, X):
                    to_x(below, z - h, j, part).start()
                to_sib(below, part).start()

            @pl.when(both(here, z + h < Z))
            def _():
                arrived(above, part)

            @pl.when(both(here, z + h < Z, z >= 1))
            def _():
                to_down(above, z + h, part).start()

            @pl.when(both(here, z + h < Z))
            def _():
                for j in range(1, X):
                    to_x(above, z + h, j, part).start()
                to_sib(above, part).start()

    def pass_on(zb, part):
        for j in range(1, X):
            b = zb * 2 * X + lax.rem(x + j, X) * 2 + c
            arrived(b, part)
            to_sib(b, part).start()

    def across_x(h, here):
        for part in parts:

            @pl.when(both(here, z >= h))
            def _():
                pass_on(z - h, part)

            if h > 0:

                @pl.when(both(here, z + h < Z))
                def _():
                    pass_on(z + h, part)

    def q_take(j):
        b = lax.rem(me + 2 * j, n)
        remote(qall, b, sib, q_sib.at[0], q_recv).wait_recv()
        q_fwd(j).start()

    loop(1, half, q_take)

    def q_other(j):
        b = lax.rem(sib + 2 * j, n)
        remote(qall, b, sib, q_sib.at[0], q_recv).wait_recv()

    loop(0, half, q_other)

    lane = lax.broadcasted_iota(jnp.int32, (1, 2 * tok), 1)
    for i in range(half):
        pair = []
        for b in (2 * i, 2 * i + 1):
            coded = qall[b, ROWS:MSG, :].astype(jnp.float32)
            pair.append(coded[0:1] * 128.0 + coded[1:2])
        key_pos[:, i * 2 * tok : (i + 1) * 2 * tok] = jnp.where(lane < tok, pair[0], pair[1])

    page_lane = lax.broadcasted_iota(jnp.int32, (1, PAGE), 1)
    for p in range(tokens // PAGE):
        tok_owner[:, p * PAGE : (p + 1) * PAGE] = jnp.where(
            page_lane < page_fill[p], page_owner[p], -1
        )

    for copy in pool_copies:
        copy.wait()

    def fold(q, k, v, allowed, m, l, acc):
        s = lax.dot_general(q, k, NT, preferred_element_type=jnp.float32) * SCALE
        s = jnp.where(allowed, s, NEG)
        new = jnp.maximum(m, jnp.max(s, axis=1, keepdims=True))
        w = jnp.exp2(s - new)
        scale = jnp.exp2(m - new)
        l = l * scale + jnp.sum(w, axis=1, keepdims=True)
        acc = acc * scale + jnp.dot(
            w.astype(jnp.bfloat16), v, preferred_element_type=jnp.float32
        )
        return new, l, acc

    def empty(rows):
        return (
            jnp.full((rows, 1), NEG, jnp.float32),
            jnp.zeros((rows, 1), jnp.float32),
            jnp.zeros((rows, HD), jnp.float32),
        )

    chunk_tok = 1024
    drows = SEQ_BLOCK * HEAD_ROWS
    row_seq = lax.broadcasted_iota(jnp.int32, (drows, 1), 0) // HEAD_ROWS
    lane16 = lax.broadcasted_iota(jnp.int32, (HEAD_ROWS, 128), 1)

    def decode_head(h):
        for k in range(1, min(Z, KVH - 1)):
            along_z(k, h == k)
            across_x(k - 1, h == k)

        hrow = pl.multiple_of(h * HEAD_ROWS, HEAD_ROWS)
        hlane = pl.ds(pl.multiple_of(h * HD, HD), HD)

        def seq_block(sb):
            first = sb * SEQ_BLOCK
            q = qall[pl.ds(first, SEQ_BLOCK), pl.ds(hrow, HEAD_ROWS), :].reshape(drows, HD)

            def chunk(t, carry):
                at = pl.ds(pl.multiple_of(t * chunk_tok, chunk_tok), chunk_tok)
                allowed = tok_owner[:, at] == row_seq + first
                return fold(q, pool_k[at, hlane], pool_v[at, hlane], allowed, *carry)

            m, l, acc = lax.fori_loop(0, tokens // chunk_tok, chunk, empty(drows))
            o = (acc / l).astype(jnp.bfloat16).reshape(SEQ_BLOCK, HEAD_ROWS, HD)
            psend[pl.ds(first, SEQ_BLOCK), pl.ds(hrow, HEAD_ROWS), :] = o
            lse = m + jnp.log2(l)
            seen = stats[pl.ds(hrow, HEAD_ROWS), :]
            for i in range(SEQ_BLOCK):
                seen = jnp.where(
                    lane16 == first + i, lse[i * HEAD_ROWS : (i + 1) * HEAD_ROWS], seen
                )
            stats[pl.ds(hrow, HEAD_ROWS), :] = seen

        loop(0, n // SEQ_BLOCK, seq_block)

    loop(0, KVH, decode_head)

    stats[...] = jnp.transpose(stats[...])
    def code(b):
        row = jnp.broadcast_to(stats[pl.ds(b, 1), :], (16, 128))
        hi = row.astype(jnp.bfloat16).astype(jnp.float32)
        mid = (row - hi).astype(jnp.bfloat16).astype(jnp.float32)
        low = row - hi - mid
        coded = jnp.where(sub16 == 0, hi, jnp.where(sub16 == 1, mid, low))
        psend[b, ROWS:MSG, :] = coded.astype(jnp.bfloat16)

    loop(0, n, code)

    def p_copy(j):
        b = lax.rem(me + j, n)
        return pltpu.make_async_remote_copy(
            src_ref=psend.at[b],
            dst_ref=precv.at[me],
            send_sem=p_send.at[j],
            recv_sem=p_recv.at[me],
            device_id={"seq": b},
            device_id_type=MESH,
        )

    loop(1, n, lambda j: p_copy(j).start())
    precv[me] = psend[me]

    prows = GROUP * tok
    pos_col = jnp.concatenate(
        [row_position(lax.broadcasted_iota(jnp.int32, (tok, 1), 0)).astype(jnp.float32)] * GROUP,
        axis=0,
    )
    blocks = 2 * X
    chunk_keys = blocks * tok
    nearest = [sorted(range(Z), key=lambda w: (abs(w - zz), w)) for zz in range(Z)]

    def prefill(k):
        zk = sum(jnp.where(z == zz, nearest[zz][k], 0) for zz in range(Z))
        for part in parts:
            for j in range(X):
                arrived(zk * blocks + 2 * j + 1 - c, part)
        at = pl.ds(zk * blocks, blocks)
        pos = key_pos[:, pl.ds(pl.multiple_of(zk * chunk_keys, chunk_keys), chunk_keys)]

        def head(h):
            lanes = pl.ds(pl.multiple_of(h * HD, HD), HD)
            q = jnp.concatenate(
                [
                    pq[:, pl.ds(pl.multiple_of((h * GROUP + g) * HD, HD), HD)]
                    for g in range(GROUP)
                ],
                axis=0,
            )
            key = all_k[at, :, lanes].reshape(chunk_keys, HD)
            value = all_v[at, :, lanes].reshape(chunk_keys, HD)
            rows = pl.ds(pl.multiple_of(h * prows, prows), prows)
            carry = empty(prows) if k == 0 else (run_max[rows], run_sum[rows], run_out[rows])
            m, l, acc = fold(q, key, value, pos <= pos_col, *carry)
            if k < Z - 1:
                run_max[rows], run_sum[rows], run_out[rows] = m, l, acc
                return
            o = (acc / l).astype(jnp.bfloat16)
            for g in range(GROUP):
                out[:, pl.ds(pl.multiple_of((h * GROUP + g) * HD, HD), HD)] = o[
                    g * tok : (g + 1) * tok
                ]

        loop(0, KVH, head)

    done = min(Z, KVH - 1) - 1
    for k in range(Z):
        if k > done:
            along_z(k, True)
            across_x(k - 1, True)
        if k == Z - 1:
            across_x(k, True)
        prefill(k)
        if k == 0 and done + 1 < Z:
            done += 1
            along_z(done, True)
            across_x(done - 1, True)

    def p_take(j):
        b = lax.rem(me + j, n)
        pltpu.make_async_remote_copy(
            src_ref=psend.at[b],
            dst_ref=precv.at[b],
            send_sem=p_send.at[0],
            recv_sem=p_recv.at[b],
            device_id={"seq": b},
            device_id_type=MESH,
        ).wait_recv()

    loop(1, n, p_take)

    def decode_stat(d):
        coded = precv[d, ROWS:MSG, :].astype(jnp.float32)
        stats_in[pl.ds(d, 1), :] = coded[0:1] + coded[1:2] + coded[2:3]

    loop(0, n, decode_stat)
    lse = jnp.transpose(stats_in[...])[0:ROWS]
    q = own_q[...]
    row_id = lax.broadcasted_iota(jnp.int32, (ROWS, 1), 0)
    row_step = (row_id // GROUP) % STEPS

    def per_row(wide, j):
        return jnp.concatenate(
            [
                jnp.broadcast_to(wide[j : j + 1, h * HD : (h + 1) * HD], (HEAD_ROWS, HD))
                for h in range(KVH)
            ],
            axis=0,
        )

    wide_k = step_k[0].astype(jnp.float32)
    wide_v = step_v[0].astype(jnp.float32)
    scores = []
    for j in range(STEPS):
        s = jnp.sum(q * per_row(wide_k, j), axis=1, keepdims=True) * SCALE
        scores.append(jnp.where(row_step >= j, s, NEG))
    top = jnp.max(lse, axis=1, keepdims=True)
    for s in scores:
        top = jnp.maximum(top, s)
    w = jnp.exp2(lse - top)
    denominator = jnp.sum(w, axis=1, keepdims=True)
    numerator = jnp.zeros((ROWS, HD), jnp.float32)
    for j in range(STEPS):
        e = jnp.exp2(scores[j] - top)
        denominator += e
        numerator += e * per_row(wide_v, j)
    dev = lax.broadcasted_iota(jnp.int32, (ROWS, 128), 1)

    def add(d, total):
        wd = jnp.sum(jnp.where(dev == d, w, 0.0), axis=1, keepdims=True)
        return total + wd * precv[d, 0:ROWS, :].astype(jnp.float32)

    numerator = lax.fori_loop(0, n, add, numerator, unroll=4)
    result = numerator / denominator
    for j in range(QH):
        for i in range(STEPS):
            r = (j // GROUP) * HEAD_ROWS + i * GROUP + j % GROUP
            own_dec[i : i + 1, j * HD : (j + 1) * HD] = result[r : r + 1]
    dec[0] = own_dec[...].astype(jnp.bfloat16)

    loop(1, half, lambda j: q_copy(j).wait_send())
    loop(0, half, lambda j: q_fwd(j).wait_send())
    loop(1, n, lambda j: p_copy(j).wait_send())
    for part in parts:
        for h in range(Z):

            @pl.when(both(z >= h, z + 1 < Z))
            def _():
                to_up(column(z - h), z - h, part).wait_send()

            @pl.when(both(z + h < Z, z >= 1))
            def _():
                to_down(column(z + h), z + h, part).wait_send()

        def left(zb):
            for j in range(1, X):
                to_x(column(zb), zb, j, part).wait_send()

        loop(0, Z, left)
        loop(0, half, lambda j: to_sib(2 * j + c, part).wait_send())


def shards(
    prompt_queries,
    prompt_keys,
    prompt_values,
    prompt_positions,
    step_queries,
    step_keys,
    step_values,
    pool_keys,
    pool_values,
    page_owner,
    page_fill,
):
    n = lax.axis_size("seq")
    X = max(1, round((n // 2) ** (1 / 3)))
    Z = n // (2 * X)
    tok = prompt_queries.shape[0]
    pages = pool_keys.shape[0]
    tokens = pages * PAGE
    vmem = pl.BlockSpec(memory_space=pltpu.VMEM)
    smem = pl.BlockSpec(memory_space=pltpu.SMEM)
    hbm = pl.BlockSpec(memory_space=pl.ANY)
    dma = pltpu.SemaphoreType.DMA
    bf16 = jnp.bfloat16
    return pl.pallas_call(
        functools.partial(kernel, n, X),
        out_shape=(
            jax.ShapeDtypeStruct((tok, QH * HD), bf16),
            jax.ShapeDtypeStruct((1, STEPS, QH * HD), bf16),
        ),
        in_specs=[smem] * 3 + [vmem] * 6 + [hbm] * 2,
        out_specs=(vmem, vmem),
        scratch_shapes=[
            pltpu.VMEM((n, MSG, HD), bf16),
            pltpu.VMEM((n, tok, KVH * HD), bf16),
            pltpu.VMEM((n, tok, KVH * HD), bf16),
            pltpu.VMEM((tokens, KVH * HD), bf16),
            pltpu.VMEM((tokens, KVH * HD), bf16),
            pltpu.VMEM((1, n * tok), jnp.float32),
            pltpu.VMEM((1, tokens), jnp.int32),
            pltpu.VMEM((n, MSG, HD), bf16),
            pltpu.VMEM((n, MSG, HD), bf16),
            pltpu.VMEM((128, 128), jnp.float32),
            pltpu.VMEM((128, 128), jnp.float32),
            pltpu.VMEM((ROWS, HD), jnp.float32),
            pltpu.VMEM((STEPS, QH * HD), jnp.float32),
            pltpu.VMEM((QH * tok, 1), jnp.float32),
            pltpu.VMEM((QH * tok, 1), jnp.float32),
            pltpu.VMEM((QH * tok, HD), jnp.float32),
            dma((2,)),
            dma((n // 2,)),
            dma((n // 2,)),
            dma((n,)),
            dma((n,)),
            dma((n,)),
            dma((2 * Z,)),
            dma((2 * Z,)),
            dma((2 * Z * X,)),
            dma((n,)),
            dma((n,)),
            dma((n,)),
        ],
        compiler_params=pltpu.CompilerParams(
            collective_id=0, has_side_effects=True, vmem_limit_bytes=56 * 1024 * 1024
        ),
    )(
        prompt_positions,
        page_owner.reshape(pages),
        page_fill,
        step_queries,
        prompt_queries,
        prompt_keys,
        prompt_values,
        step_keys,
        step_values,
        pool_keys.reshape(tokens, KVH * HD),
        pool_values.reshape(tokens, KVH * HD),
    )


def solution(mesh):
    rows = P(("group", "seq"), None)
    flat = P(("group", "seq"))
    cube = P(("group", "seq"), None, None)
    in_specs = (rows, rows, rows, flat, cube, cube, cube, cube, cube, rows, flat)
    return jax.shard_map(
        shards, mesh=mesh, in_specs=in_specs, out_specs=(rows, cube), check_vma=False
    )
```

time: 51.9 us -> 56.2 us (1.083); the launches traced: 51.5 us -> 55.1 us
  Pallas kernels: 40 us -> 51.3 us
  local copies, waits for them, and re-layouts: 7.33 us -> 3.2 us
  other arithmetic: 3.51 us -> 0 us
    pallas_call x1, Pallas kernels: 40 us -> 51.3 us  [shards(): pl.pallas_call(functools.partial(kernel, n, X), out_shape=(jax.ShapeDtype...]
    broadcast_in_dim x6 -> x0, local copies, waits for them, and re-layouts: 3.32 us -> none  [the longest x4 2.64 us: per_row(): jnp.broadcast_to(a, (STEPS, KVH, HEAD_ROWS, HD)).reshape(STEPS, ROWS, HD)]
    select_n x1 -> x0, other arithmetic: 1.35 us -> none  [shards(): tok_owner = jnp.where(valid, page_owner, -1).reshape(1, tokens)]
    another operation x2 -> x0, other arithmetic: 0.82 us -> none
    transpose x1 -> x0, local copies, waits for them, and re-layouts: 0.72 us -> none  [shards(): decode_out = jnp.transpose(dec.reshape(KVH, STEPS, GROUP, HD), (1, 0, 2, 3))]
    concatenate x1 -> x0, other arithmetic: 0.68 us -> none  [shards(): qmsg = jnp.concatenate([rows, coded.astype(jnp.bfloat16)])]
    convert_element_type x1 -> x0, other arithmetic: 0.66 us -> none  [shards(): prompt_positions.astype(jnp.float32)[:, None]]
    reshape x2 -> x0, local copies, waits for them, and re-layouts: 0.62 us -> none  [the longest x1 0.62 us: shards(): return (prefill_out, decode_out.reshape(1, STEPS, QH * HD))]
where the time goes in v2:
time: 56.2 us; the launch traced here: 55.1 us
  Pallas kernels  51.3 us (91%)
  local copies, waits for them, and re-layouts  3.2 us (6%)
  between operations  0.64 us (1%)
    pallas_call x1, Pallas kernels, shards(): pl.pallas_call(functools.partial(kernel, n, X), out_shape=(jax.ShapeDtype...  51.3 us
    unnamed x2, local copies, waits for them, and re-layouts  3.2 us

profile of v2, /device:TPU:1, one launch (start us, length us, event | category | flops | bytes accessed | tf_op | source)
XLA Modules:
  0.0 55.1 jit_solution(3252645678638848069)
XLA Ops:
  0.6 51.3 %shard_map.122 = (bf16[64,4096]{1,0:T(8,128)(2,1)}, bf16[1,2,4096]{2,1,0:T(2,128)(2,1)}) custom-call(s32[64]{0:T(128)} %positions.1, s32[32]{0:T(128)} %bitcast.5, s32[32]{0:T(128)} %page_fill.1, bf16[1,2,4096]{2,1,0:T(2,128)(2,1)} %step_q.1, bf16[64,4096]{1,0:T(8,128)(2,1)} %pq.1, bf16[64,512]{1,0:T(8,128)(2,1)} %own_k.1, bf16[64,512]{1,0:T(8,128)(2,1)} %own_v.1, ...), custom_call_target="tpu_custom_call" | custom-call | tf_op jit(solution)/shard_map/pallas_call | solution.py:513
  51.9 1.9 %copy.15 = bf16[64,4096]{1,0:T(8,128)(2,1)} copy(bf16[64,4096]{1,0:T(8,128)(2,1)} %get-tuple-element.4) | data formatting | bytes 1048576
  53.8 1.3 %copy.16 = bf16[1,2,4096]{2,1,0:T(2,128)(2,1)} copy(bf16[1,2,4096]{2,1,0:T(2,128)(2,1)} %get-tuple-element.5) | data formatting | bytes 32768

commit v3 on v2

--- a/solution.py
+++ b/solution.py
@@ -52,9 +52,6 @@
     stats_in,
     own_q,
     own_dec,
-    run_max,
-    run_sum,
-    run_out,
     pool_sem,
     q_send,
     q_sib,
@@ -76,7 +73,6 @@
     z = me // (2 * X)
     sib = me + 1 - 2 * c
     tok = own_k.shape[0]
-    keys = n * tok
     tokens = pool_k.shape[0]
 
     pool_copies = [
@@ -171,20 +167,6 @@
         bits = [jnp.where(one, 1, 0) for one in conditions]
         return functools.reduce(lambda p, q: p * q, bits) == 1
 
-    for part in parts:
-
-        @pl.when(z + 1 < Z)
-        def _():
-            to_up(me, z, part).start()
-
-        @pl.when(z >= 1)
-        def _():
-            to_down(me, z, part).start()
-
-        for j in range(1, X):
-            to_x(me, z, j, part).start()
-        to_sib(me, part).start()
-
     def along_z(h, here):
         below, above = column(z - h), column(z + h)
         for part in parts:
@@ -242,6 +224,20 @@
         q_fwd(j).start()
 
     loop(1, half, q_take)
+
+    for part in parts:
+
+        @pl.when(z + 1 < Z)
+        def _():
+            to_up(me, z, part).start()
+
+        @pl.when(z >= 1)
+        def _():
+            to_down(me, z, part).start()
+
+        for j in range(1, X):
+            to_x(me, z, j, part).start()
+        to_sib(me, part).start()
 
     def q_other(j):
         b = lax.rem(sib + 2 * j, n)
@@ -266,32 +262,24 @@
     for copy in pool_copies:
         copy.wait()
 
-    def fold(q, k, v, allowed, m, l, acc):
+    def fold(q, k, v, allowed, m, acc):
         s = lax.dot_general(q, k, NT, preferred_element_type=jnp.float32) * SCALE
         s = jnp.where(allowed, s, NEG)
-        new = jnp.maximum(m, jnp.max(s, axis=1, keepdims=True))
-        w = jnp.exp2(s - new)
-        scale = jnp.exp2(m - new)
-        l = l * scale + jnp.sum(w, axis=1, keepdims=True)
-        acc = acc * scale + jnp.dot(
-            w.astype(jnp.bfloat16), v, preferred_element_type=jnp.float32
-        )
-        return new, l, acc
-
-    def empty(rows):
-        return (
-            jnp.full((rows, 1), NEG, jnp.float32),
-            jnp.zeros((rows, 1), jnp.float32),
-            jnp.zeros((rows, HD), jnp.float32),
-        )
-
-    chunk_tok = 1024
+        new = jnp.max(s, axis=1, keepdims=True)
+        if m is not None:
+            new = jnp.maximum(m, new)
+        w = jnp.exp2(s - new).astype(jnp.bfloat16)
+        wide = jnp.concatenate([v, jnp.ones_like(v)], axis=1)
+        more = jnp.dot(w, wide, preferred_element_type=jnp.float32)
+        return new, more if m is None else acc * jnp.exp2(m - new) + more
+
+    chunk_tok = 512
     drows = SEQ_BLOCK * HEAD_ROWS
     row_seq = lax.broadcasted_iota(jnp.int32, (drows, 1), 0) // HEAD_ROWS
     lane16 = lax.broadcasted_iota(jnp.int32, (HEAD_ROWS, 128), 1)
 
     def decode_head(h):
-        for k in range(1, min(Z, KVH - 1)):
+        for k in range(1, min(Z, KVH)):
             along_z(k, h == k)
             across_x(k - 1, h == k)
 
@@ -303,12 +291,16 @@
             q = qall[pl.ds(first, SEQ_BLOCK), pl.ds(hrow, HEAD_ROWS), :].reshape(drows, HD)
 
             def chunk(t, carry):
-                at = pl.ds(pl.multiple_of(t * chunk_tok, chunk_tok), chunk_tok)
+                at = pl.ds(t * chunk_tok, chunk_tok)
                 allowed = tok_owner[:, at] == row_seq + first
                 return fold(q, pool_k[at, hlane], pool_v[at, hlane], allowed, *carry)
 
-            m, l, acc = lax.fori_loop(0, tokens // chunk_tok, chunk, empty(drows))
-            o = (acc / l).astype(jnp.bfloat16).reshape(SEQ_BLOCK, HEAD_ROWS, HD)
+            carry = (None, None)
+            for t in range(tokens // chunk_tok):
+                carry = chunk(t, carry)
+            m, acc = carry
+            l = acc[:, HD : HD + 1]
+            o = (acc[:, :HD] / acc[:, HD:]).astype(jnp.bfloat16).reshape(SEQ_BLOCK, HEAD_ROWS, HD)
             psend[pl.ds(first, SEQ_BLOCK), pl.ds(hrow, HEAD_ROWS), :] = o
             lse = m + jnp.log2(l)
             seen = stats[pl.ds(hrow, HEAD_ROWS), :]
@@ -347,60 +339,45 @@
     loop(1, n, lambda j: p_copy(j).start())
     precv[me] = psend[me]
 
-    prows = GROUP * tok
+    for h in range(min(Z, KVH), Z):
+        along_z(h, True)
+        across_x(h - 1, True)
+    across_x(Z - 1, True)
+
+    def kv_other(j):
+        for part in parts:
+            arrived(2 * j + 1 - c, part)
+
+    loop(0, half, kv_other)
+
+    fan = 8
     pos_col = jnp.concatenate(
-        [row_position(lax.broadcasted_iota(jnp.int32, (tok, 1), 0)).astype(jnp.float32)] * GROUP,
+        [row_position(lax.broadcasted_iota(jnp.int32, (tok, 1), 0)).astype(jnp.float32)] * fan,
         axis=0,
     )
-    blocks = 2 * X
-    chunk_keys = blocks * tok
-    nearest = [sorted(range(Z), key=lambda w: (abs(w - zz), w)) for zz in range(Z)]
-
-    def prefill(k):
-        zk = sum(jnp.where(z == zz, nearest[zz][k], 0) for zz in range(Z))
-        for part in parts:
-            for j in range(X):
-                arrived(zk * blocks + 2 * j + 1 - c, part)
-        at = pl.ds(zk * blocks, blocks)
-        pos = key_pos[:, pl.ds(pl.multiple_of(zk * chunk_keys, chunk_keys), chunk_keys)]
-
-        def head(h):
-            lanes = pl.ds(pl.multiple_of(h * HD, HD), HD)
-            q = jnp.concatenate(
-                [
-                    pq[:, pl.ds(pl.multiple_of((h * GROUP + g) * HD, HD), HD)]
-                    for g in range(GROUP)
-                ],
-                axis=0,
-            )
+    chunk_keys = 1024
+    blocks = chunk_keys // tok
+
+    def prefill(u):
+        h = u // (GROUP // fan)
+        lanes = pl.ds(pl.multiple_of(h * HD, HD), HD)
+        q = jnp.concatenate(
+            [pq[:, pl.ds(pl.multiple_of((u * fan + g) * HD, HD), HD)] for g in range(fan)],
+            axis=0,
+        )
+        carry = (None, None)
+        for t in range(n * tok // chunk_keys):
+            at = pl.ds(t * blocks, blocks)
             key = all_k[at, :, lanes].reshape(chunk_keys, HD)
             value = all_v[at, :, lanes].reshape(chunk_keys, HD)
-            rows = pl.ds(pl.multiple_of(h * prows, prows), prows)
-            carry = empty(prows) if k == 0 else (run_max[rows], run_sum[rows], run_out[rows])
-            m, l, acc = fold(q, key, value, pos <= pos_col, *carry)
-            if k < Z - 1:
-                run_max[rows], run_sum[rows], run_out[rows] = m, l, acc
-                return
-            o = (acc / l).astype(jnp.bfloat16)
-            for g in range(GROUP):
-                out[:, pl.ds(pl.multiple_of((h * GROUP + g) * HD, HD), HD)] = o[
-                    g * tok : (g + 1) * tok
-                ]
-
-        loop(0, KVH, head)
-
-    done = min(Z, KVH - 1) - 1
-    for k in range(Z):
-        if k > done:
-            along_z(k, True)
-            across_x(k - 1, True)
-        if k == Z - 1:
-            across_x(k, True)
-        prefill(k)
-        if k == 0 and done + 1 < Z:
-            done += 1
-            along_z(done, True)
-            across_x(done - 1, True)
+            pos = key_pos[:, pl.ds(t * chunk_keys, chunk_keys)]
+            carry = fold(q, key, value, pos <= pos_col, *carry)
+        acc = carry[1]
+        o = (acc[:, :HD] / acc[:, HD:]).astype(jnp.bfloat16)
+        for g in range(fan):
+            out[:, pl.ds(pl.multiple_of((u * fan + g) * HD, HD), HD)] = o[g * tok : (g + 1) * tok]
+
+    loop(0, QH // fan, prefill)
 
     def p_take(j):
         b = lax.rem(me + j, n)
@@ -532,9 +509,6 @@
             pltpu.VMEM((128, 128), jnp.float32),
             pltpu.VMEM((ROWS, HD), jnp.float32),
             pltpu.VMEM((STEPS, QH * HD), jnp.float32),
-            pltpu.VMEM((QH * tok, 1), jnp.float32),
-            pltpu.VMEM((QH * tok, 1), jnp.float32),
-            pltpu.VMEM((QH * tok, HD), jnp.float32),
             dma((2,)),
             dma((n // 2,)),
             dma((n // 2,)),

time: 56.2 us -> 41.9 us (0.75); the launches traced: 55.1 us -> 41.7 us
  Pallas kernels: 51.3 us -> 37.8 us
    pallas_call x1, Pallas kernels: 51.3 us -> 37.8 us  [shards(): pl.pallas_call(functools.partial(kernel, n, X), out_shape=(jax.ShapeDtype...]
where the time goes in v3:
time: 41.9 us; the launch traced here: 41.7 us
  Pallas kernels  37.8 us (90%)
  local copies, waits for them, and re-layouts  3.2 us (8%)
  between operations  0.64 us (2%)
    pallas_call x1, Pallas kernels, shards(): pl.pallas_call(functools.partial(kernel, n, X), out_shape=(jax.ShapeDtype...  37.8 us
    unnamed x2, local copies, waits for them, and re-layouts  3.2 us

profile of v3, /device:TPU:1, one launch (start us, length us, event | category | flops | bytes accessed | tf_op | source)
XLA Modules:
  0.0 41.7 jit_solution(15291311513209490853)
XLA Ops:
  0.6 37.8 %shard_map.122 = (bf16[64,4096]{1,0:T(8,128)(2,1)}, bf16[1,2,4096]{2,1,0:T(2,128)(2,1)}) custom-call(s32[64]{0:T(128)} %positions.1, s32[32]{0:T(128)} %bitcast.5, s32[32]{0:T(128)} %page_fill.1, bf16[1,2,4096]{2,1,0:T(2,128)(2,1)} %step_q.1, bf16[64,4096]{1,0:T(8,128)(2,1)} %pq.1, bf16[64,512]{1,0:T(8,128)(2,1)} %own_k.1, bf16[64,512]{1,0:T(8,128)(2,1)} %own_v.1, ...), custom_call_target="tpu_custom_call" | custom-call | tf_op jit(solution)/shard_map/pallas_call | solution.py:490
  38.5 1.9 %copy.15 = bf16[64,4096]{1,0:T(8,128)(2,1)} copy(bf16[64,4096]{1,0:T(8,128)(2,1)} %get-tuple-element.4) | data formatting | bytes 1048576
  40.4 1.3 %copy.16 = bf16[1,2,4096]{2,1,0:T(2,128)(2,1)} copy(bf16[1,2,4096]{2,1,0:T(2,128)(2,1)} %get-tuple-element.5) | data formatting | bytes 32768

commit v4 on v3

--- a/solution.py
+++ b/solution.py
@@ -52,6 +52,8 @@
     stats_in,
     own_q,
     own_dec,
+    run_max,
+    run_out,
     pool_sem,
     q_send,
     q_sib,
@@ -312,7 +314,8 @@
 
         loop(0, n // SEQ_BLOCK, seq_block)
 
-    loop(0, KVH, decode_head)
+    for h in range(KVH):
+        decode_head(h)
 
     stats[...] = jnp.transpose(stats[...])
     def code(b):
@@ -342,42 +345,59 @@
     for h in range(min(Z, KVH), Z):
         along_z(h, True)
         across_x(h - 1, True)
-    across_x(Z - 1, True)
-
-    def kv_other(j):
-        for part in parts:
-            arrived(2 * j + 1 - c, part)
-
-    loop(0, half, kv_other)
+
+    def kv_other(side):
+        def take(j):
+            for part in parts:
+                arrived(side * half + 2 * j + 1 - c, part)
+
+        loop(0, half // 2, take)
 
     fan = 8
     pos_col = jnp.concatenate(
         [row_position(lax.broadcasted_iota(jnp.int32, (tok, 1), 0)).astype(jnp.float32)] * fan,
         axis=0,
     )
-    chunk_keys = 1024
+    chunk_keys = 512
     blocks = chunk_keys // tok
 
-    def prefill(u):
+    side_keys = half * tok
+
+    def prefill(u, side, last):
         h = u // (GROUP // fan)
         lanes = pl.ds(pl.multiple_of(h * HD, HD), HD)
+        rows = pl.ds(u * fan * tok, fan * tok)
         q = jnp.concatenate(
             [pq[:, pl.ds(pl.multiple_of((u * fan + g) * HD, HD), HD)] for g in range(fan)],
             axis=0,
         )
-        carry = (None, None)
-        for t in range(n * tok // chunk_keys):
-            at = pl.ds(t * blocks, blocks)
+        carry = (run_max[rows, 0:1], run_out[rows]) if last else (None, None)
+        for t in range(side_keys // chunk_keys):
+            at = pl.ds(side * half + t * blocks, blocks)
             key = all_k[at, :, lanes].reshape(chunk_keys, HD)
             value = all_v[at, :, lanes].reshape(chunk_keys, HD)
-            pos = key_pos[:, pl.ds(t * chunk_keys, chunk_keys)]
+            first = pl.multiple_of(side * side_keys + t * chunk_keys, chunk_keys)
+            pos = key_pos[:, pl.ds(first, chunk_keys)]
             carry = fold(q, key, value, pos <= pos_col, *carry)
-        acc = carry[1]
+        m, acc = carry
+        if not last:
+            run_max[rows] = jnp.broadcast_to(m, (fan * tok, HD))
+            run_out[rows] = acc
+            return
         o = (acc[:, :HD] / acc[:, HD:]).astype(jnp.bfloat16)
         for g in range(fan):
             out[:, pl.ds(pl.multiple_of((u * fan + g) * HD, HD), HD)] = o[g * tok : (g + 1) * tok]
 
-    loop(0, QH // fan, prefill)
+    near = z // (Z // 2)
+    kv_other(near)
+    units = QH // fan
+    for u in range(units):
+        prefill(u, near, False)
+        if u == 1:
+            across_x(Z - 1, True)
+    kv_other(1 - near)
+    for u in range(units):
+        prefill(u, 1 - near, True)
 
     def p_take(j):
         b = lax.rem(me + j, n)
@@ -509,6 +529,8 @@
             pltpu.VMEM((128, 128), jnp.float32),
             pltpu.VMEM((ROWS, HD), jnp.float32),
             pltpu.VMEM((STEPS, QH * HD), jnp.float32),
+            pltpu.VMEM((QH * tok, HD), jnp.float32),
+            pltpu.VMEM((QH * tok, 2 * HD), jnp.float32),
             dma((2,)),
             dma((n // 2,)),
             dma((n // 2,)),

time: 41.9 us -> 40.3 us (0.962)
  Pallas kernels: 37.8 us -> 36 us
    pallas_call x1, Pallas kernels: 37.8 us -> 36 us  [shards(): pl.pallas_call(functools.partial(kernel, n, X), out_shape=(jax.ShapeDtype...]
where the time goes in v4:
time: 40.3 us; the launch traced here: 39.8 us
  Pallas kernels  36 us (89%)
  local copies, waits for them, and re-layouts  3.2 us (8%)
  between operations  0.64 us (2%)
    pallas_call x1, Pallas kernels, shards(): pl.pallas_call(functools.partial(kernel, n, X), out_shape=(jax.ShapeDtype...  36 us
    unnamed x2, local copies, waits for them, and re-layouts  3.2 us

profile of v4, /device:TPU:1, one launch (start us, length us, event | category | flops | bytes accessed | tf_op | source)
XLA Modules:
  0.0 39.8 jit_solution(3377714238335677129)
XLA Ops:
  0.6 36.0 %shard_map.122 = (bf16[64,4096]{1,0:T(8,128)(2,1)}, bf16[1,2,4096]{2,1,0:T(2,128)(2,1)}) custom-call(s32[64]{0:T(128)} %positions.1, s32[32]{0:T(128)} %bitcast.5, s32[32]{0:T(128)} %page_fill.1, bf16[1,2,4096]{2,1,0:T(2,128)(2,1)} %step_q.1, bf16[64,4096]{1,0:T(8,128)(2,1)} %pq.1, bf16[64,512]{1,0:T(8,128)(2,1)} %own_k.1, bf16[64,512]{1,0:T(8,128)(2,1)} %own_v.1, ...), custom_call_target="tpu_custom_call" | custom-call | tf_op jit(solution)/shard_map/pallas_call | solution.py:510
  36.6 1.9 %copy.15 = bf16[64,4096]{1,0:T(8,128)(2,1)} copy(bf16[64,4096]{1,0:T(8,128)(2,1)} %get-tuple-element.4) | data formatting | bytes 1048576
  38.5 1.3 %copy.16 = bf16[1,2,4096]{2,1,0:T(2,128)(2,1)} copy(bf16[1,2,4096]{2,1,0:T(2,128)(2,1)} %get-tuple-element.5) | data formatting | bytes 32768
